TPU v7x, 32 devices: a whole 2x2x4 slice. The times are simulated.
32 devices in a mesh: wake: 16 (over z, y, core), col: 2 (over x).
Axes of the slice: x: 2, y: 2, z: 4, core: 2. Of those that a mesh axis runs over, the one named last changes fastest.
Arguments:
- points: float32 [3, 32768], P(None, ('wake', 'col')), may hold values from -6 to 6
- normals: float32 [3, 32768], P(None, ('wake', 'col')), may hold values from -6 to 6
- freestream: float32 [3], replicated, may hold values from -2 to 2
- wake_nodes: float32 [3, 16384], P(None, 'wake'), may hold values from -6 to 6
- circulation: float32 [16384], P('wake'), may hold values from -4 to 4
- filament: int32 [16384], P('wake'), may hold values from 0 to 127, never falling along the last dimension, each value on 1 to 256 neighbouring positions
- self_term: float32 [32768], P(('wake', 'col')), may hold values from 1 to 8
- near_blocks: float32 [256, 2, 1, 128, 128], P('wake', 'col'), may hold values from -0.5 to 0.5
- near_index: int32 [256, 2, 1], P('wake', 'col'), may hold values from 0 to 127
- far_left: float32 [2, 32, 32768], P('col', None, 'wake'), may hold values from -1 to 1
- far_right: float32 [16, 32, 32768], P('wake', None, 'col'), may hold values from -0.046875 to 0.046875
Outputs:
- right_side: float32 [32768], P(('wake', 'col'))
- strengths: float32 [32768], P(('wake', 'col'))
Inputs may be any that keep to these rules, and one draw needn't show every extreme that they name: Filament numbers never fall along the nodes; each filament has 1 to 256 nodes and one has exactly 256.
All inputs are finite; a program needn't handle non-finite values.
Results may differ from a plain program's by a relative error of at most 0.0004.
Values sent between devices are 32-bit elements; how exact they have to be, the bound alone decides.
No kernel may reach another device: no remote copies, remote signals or barrier semaphores. Data moves between devices by JAX's collectives and lax.ppermute only.
A program may use at most 64 MiB of HBM per device.

v0:
```python
import math
import jax
import jax.numpy as jnp
from jax import lax
from jax.sharding import PartitionSpec as P

KRYLOV = 6
core_sq = 0.01
four_pi = 4.0 * math.pi


def shifted(value, axis, steps):
    count = lax.axis_size(axis)
    first, last = (max(0, -steps), min(count, count - steps))
    return lax.ppermute(value, axis, [(source, source + steps) for source in range(first, last)])


def induce(points, normals, segments):
    near_arm = points[:, :, None] - segments[0:3, None, :]
    far_arm = points[:, :, None] - segments[3:6, None, :]
    cross_x = near_arm[1] * far_arm[2] - near_arm[2] * far_arm[1]
    cross_y = near_arm[2] * far_arm[0] - near_arm[0] * far_arm[2]
    cross_z = near_arm[0] * far_arm[1] - near_arm[1] * far_arm[0]
    normal_part = (
        cross_x * normals[0][:, None]
        + cross_y * normals[1][:, None]
        + cross_z * normals[2][:, None]
    )
    near_len = jnp.sqrt(jnp.sum(near_arm * near_arm, axis=0))
    far_len = jnp.sqrt(jnp.sum(far_arm * far_arm, axis=0))
    inner_dot = jnp.sum(near_arm * far_arm, axis=0)
    factor = (
        segments[6][None, :]
        * (near_len + far_len)
        / (four_pi * (near_len * far_len * (near_len * far_len + inner_dot) + core_sq))
    )
    return jnp.sum(factor * normal_part, axis=1)


def small_solve(gram_matrix, projected):
    size_now = gram_matrix.shape[0]
    factor = [[None for inner_pos in range(size_now)] for outer_pos in range(size_now)]
    for outer_pos in range(size_now):
        for inner_pos in range(outer_pos + 1):
            partial_sum = gram_matrix[outer_pos, inner_pos]
            for middle in range(inner_pos):
                partial_sum = partial_sum - factor[outer_pos][middle] * factor[inner_pos][middle]
            if inner_pos == outer_pos:
                factor[outer_pos][inner_pos] = jnp.sqrt(partial_sum)
            else:
                factor[outer_pos][inner_pos] = partial_sum / factor[inner_pos][inner_pos]
    forward = []
    for outer_pos in range(size_now):
        partial_sum = projected[outer_pos]
        for middle in range(outer_pos):
            partial_sum = partial_sum - factor[outer_pos][middle] * forward[middle]
        forward.append(partial_sum / factor[outer_pos][outer_pos])
    backward = [None for outer_pos in range(size_now)]
    for outer_pos in reversed(range(size_now)):
        partial_sum = forward[outer_pos]
        for middle in range(outer_pos + 1, size_now):
            partial_sum = partial_sum - factor[middle][outer_pos] * backward[middle]
        backward[outer_pos] = partial_sum / factor[outer_pos][outer_pos]
    return backward


def body(
    points,
    normals,
    freestream,
    wake_nodes,
    circulation,
    filament,
    self_term,
    near_blocks,
    near_index,
    far_left,
    far_right,
):
    highest = lax.Precision.HIGHEST
    piece_len = points.shape[1]
    filament_tag = filament.astype(jnp.float32) + 1.0
    first_node = jnp.concatenate([wake_nodes[:, 0], filament_tag[0:1]])
    following = shifted(first_node, "wake", -1)
    end_points = jnp.concatenate([wake_nodes[:, 1:], following[0:3, None]], axis=1)
    next_tag = jnp.concatenate([filament_tag[1:], following[3:4]])
    link_mask = (filament_tag == next_tag).astype(jnp.float32)
    segments = jnp.concatenate([wake_nodes, end_points, (circulation * link_mask)[None, :]], axis=0)
    shard_segs = lax.all_gather(segments, "wake", axis=1, tiled=True)
    seg_count = shard_segs.shape[1]
    add_block_len = math.gcd(seg_count, 512)

    def add_block(position, running):
        segment_block = lax.dynamic_slice_in_dim(
            shard_segs, position * add_block_len, add_block_len, 1
        )
        return running + induce(points, normals, segment_block)

    induced = lax.fori_loop(
        0, seg_count // add_block_len, add_block, jnp.zeros((piece_len,), jnp.float32)
    )
    right_side = -(jnp.dot(freestream, normals, precision=highest) + induced)
    block_len = near_blocks.shape[-1]
    local_blocks = near_blocks[:, 0]
    local_index = near_index[:, 0]
    left_factor = far_left[0]
    right_factor = far_right[0]
    initial_sq = lax.psum(jnp.sum(right_side * right_side), ("wake", "col"))
    initial_norm = jnp.sqrt(initial_sq)
    krylov = [right_side / initial_norm]
    hessenberg = jnp.zeros((KRYLOV + 1, KRYLOV), jnp.float32)
    for column in range(KRYLOV):
        vector = krylov[column]
        column_vec = lax.all_gather(vector, "wake", axis=0, tiled=True)
        far_coeff = jnp.dot(right_factor, column_vec, precision=highest)
        column_blocks = column_vec.reshape(-1, block_len)
        selected = column_blocks[local_index]
        near_part = jnp.einsum("rkij,rkj->ri", local_blocks, selected, precision=highest).reshape(
            piece_len * lax.axis_size("col")
        )
        summed = lax.psum_scatter(
            near_part + jnp.dot(far_coeff, left_factor, precision=highest),
            "col",
            scatter_dimension=0,
            tiled=True,
        )
        image_vec = self_term * vector + summed
        local_dots = jnp.stack([jnp.sum(image_vec * member) for member in krylov])
        coeffs = lax.psum(local_dots, ("wake", "col"))
        remainder = image_vec
        for position in range(column + 1):
            remainder = remainder - coeffs[position] * krylov[position]
        new_norm = jnp.sqrt(lax.psum(jnp.sum(remainder * remainder), ("wake", "col")))
        hessenberg = (
            hessenberg.at[: column + 1, column].set(coeffs).at[column + 1, column].set(new_norm)
        )
        if column + 1 < KRYLOV:
            krylov.append(remainder / new_norm)
    gram_matrix = jnp.dot(hessenberg.T, hessenberg, precision=highest)
    combination = small_solve(gram_matrix, initial_norm * hessenberg[0])
    strengths = combination[0] * krylov[0]
    for position in range(1, KRYLOV):
        strengths = strengths + combination[position] * krylov[position]
    return (right_side, strengths)


def solution(mesh):
    in_specs = (
        P(None, ("wake", "col")),
        P(None, ("wake", "col")),
        P(),
        P(None, "wake"),
        P("wake"),
        P("wake"),
        P(("wake", "col")),
        P("wake", "col", None, None, None),
        P("wake", "col", None),
        P("col", None, "wake"),
        P("wake", None, "col"),
    )
    out_specs = (P(("wake", "col")), P(("wake", "col")))
    return jax.shard_map(body, mesh=mesh, in_specs=in_specs, out_specs=out_specs, check_vma=False)
```

profile of v0, /device:TPU:0, one launch (start us, length us, event | category | flops | bytes accessed | tf_op | source)
XLA Modules:
  0.0 1426.7 jit_solution(15136460085953510115)
XLA Ops:
  18.1 26.6 %all_gather.21 = f32[7,16384]{1,0:T(8,128)} all-gather(f32[7,1024]{1,0:T(8,128)S(1)} %pad_maximum_fusion), channel_id=1, replica_groups=mesh['wake'=16,'col'=2] {'wake'}, dimensions={1}, use_global_device_ids=true | all-gather | bytes 487424 | tf_op jit(solution)/shard_map/all_gather | solution.py:89
  44.7 603.5 %while.26 = (s32[]{:T(128)}, f32[1024]{0:T(1024)S(1)}, f32[7,16384]{1,0:T(8,128)}, f32[3,1024]{1,0:T(4,128)}, f32[3,1024]{1,0:T(4,128)}, /*index=5*/s32[]{:T(128...) while((s32[]{:T(128)}, f32[1024]{0:T(1024)S(1)}, f32[7,16384]{1,0:T(8,128)}, ...), condition=%wide.region_5.0_spmd.clone, body=%wide.region_0.0_spmd.clone.sunk | while | flops 23593992 | bytes 37906656 | solution.py:99
  45.6 9.2 multiply_reduce_fusion.32
  55.6 7.9 fusion.107
  64.4 9.2 multiply_reduce_fusion.32
  74.4 7.9 fusion.107
  83.3 9.2 multiply_reduce_fusion.32
  102.1 9.2 multiply_reduce_fusion.32
  112.2 7.9 fusion.107
  121.0 9.2 multiply_reduce_fusion.32
  139.9 9.2 multiply_reduce_fusion.32
  158.7 9.2 multiply_reduce_fusion.32
  177.6 9.2 multiply_reduce_fusion.32
  196.4 9.2 multiply_reduce_fusion.32
  206.5 7.9 fusion.107
  215.3 9.2 multiply_reduce_fusion.32
  234.2 9.2 multiply_reduce_fusion.32
  253.0 9.2 multiply_reduce_fusion.32
  263.0 7.9 fusion.107
  271.9 9.2 multiply_reduce_fusion.32
  290.7 9.2 multiply_reduce_fusion.32
  309.6 9.2 multiply_reduce_fusion.32
  319.6 7.9 fusion.107
  328.5 9.2 multiply_reduce_fusion.32
  347.3 9.2 multiply_reduce_fusion.32
  357.3 7.9 fusion.107
  366.2 9.2 multiply_reduce_fusion.32
  385.0 9.2 multiply_reduce_fusion.32
  403.9 9.2 multiply_reduce_fusion.32
  413.9 7.9 fusion.107
  422.7 9.2 multiply_reduce_fusion.32
  441.6 9.2 multiply_reduce_fusion.32
  460.5 9.2 multiply_reduce_fusion.32
  470.5 7.9 fusion.107
  479.3 9.2 multiply_reduce_fusion.32
  498.2 9.2 multiply_reduce_fusion.32
  517.0 9.2 multiply_reduce_fusion.32
  535.9 9.2 multiply_reduce_fusion.32
  554.8 9.2 multiply_reduce_fusion.32
  564.8 7.9 fusion.107
  573.6 9.2 multiply_reduce_fusion.32
  592.5 9.2 multiply_reduce_fusion.32
  611.3 9.2 multiply_reduce_fusion.32
  621.4 7.9 fusion.107
  630.2 9.2 multiply_reduce_fusion.32
  649.3 37.1 %psum.91 = f32[]{:T(128)} all-reduce(f32[]{:T(128)} %multiply_reduce_fusion.30), channel_id=1, replica_groups=mesh['wake'=16,'col'=2] {'wake','col'}, use_global_device_ids=true, to_apply=%region_7.0 | all-reduce | flops 1 | bytes 8 | tf_op jit(solution)/shard_map/psum | solution.py:108
  687.8 21.4 %all_gather.22 = f32[16384]{0:T(1024)S(1)} all-gather(f32[1024]{0:T(1024)S(1)} %get-tuple-element.307), channel_id=1, replica_groups=mesh['wake'=16,'col'=2] {'wake'}, dimensions={0}, use_global_device_ids=true | all-gather | bytes 69632 | tf_op jit(solution)/shard_map/all_gather | solution.py:114
  719.1 37.1 %psum.92 = f32[1]{0:T(128)} all-reduce(f32[1]{0:T(128)} %bitcast.18), channel_id=1, replica_groups=mesh['wake'=16,'col'=2] {'wake','col'}, use_global_device_ids=true, to_apply=%region_10.0 | all-reduce | flops 1 | bytes 8 | tf_op jit(solution)/shard_map/psum | solution.py:129
  757.5 42.8 %psum.93 = f32[]{:T(128)} all-reduce(f32[]{:T(128)} %get-tuple-element.305), channel_id=1, replica_groups=mesh['wake'=16,'col'=2] {'wake','col'}, use_global_device_ids=true, to_apply=%region_12.0 | all-reduce | flops 1 | bytes 8 | tf_op jit(solution)/shard_map/psum | solution.py:133
  800.9 21.2 %all_gather.23 = f32[16384]{0:T(1024)S(1)} all-gather(f32[1024]{0:T(1024)S(1)} %broadcast_divide_fusion.4), channel_id=1, replica_groups=mesh['wake'=16,'col'=2] {'wake'}, dimensions={0}, use_global_device_ids=true | all-gather | bytes 69632 | tf_op jit(solution)/shard_map/all_gather | solution.py:114
  834.1 36.8 %psum.94 = f32[2]{0:T(128)S(1)} all-reduce(f32[2]{0:T(128)S(1)} %pad_maximum_fusion.2), channel_id=1, replica_groups=mesh['wake'=16,'col'=2] {'wake','col'}, use_global_device_ids=true, to_apply=%region_17.0 | all-reduce | flops 2 | bytes 16 | tf_op jit(solution)/shard_map/psum | solution.py:129
  873.4 41.5 %psum.95 = f32[]{:T(128)} all-reduce(f32[]{:T(128)} %get-tuple-element.302), channel_id=1, replica_groups=mesh['wake'=16,'col'=2] {'wake','col'}, use_global_device_ids=true, to_apply=%region_19.0 | all-reduce | flops 1 | bytes 8 | tf_op jit(solution)/shard_map/psum | solution.py:133
  915.7 20.8 %all_gather.24 = f32[16384]{0:T(1024)S(1)} all-gather(f32[1024]{0:T(1024)S(1)} %broadcast_divide_fusion.3), channel_id=1, replica_groups=mesh['wake'=16,'col'=2] {'wake'}, dimensions={0}, use_global_device_ids=true | all-gather | bytes 69632 | tf_op jit(solution)/shard_map/all_gather | solution.py:114
  948.4 36.9 %psum.96 = f32[3]{0:T(128)S(1)} all-reduce(f32[3]{0:T(128)S(1)} %pad_maximum_fusion.3), channel_id=1, replica_groups=mesh['wake'=16,'col'=2] {'wake','col'}, use_global_device_ids=true, to_apply=%region_25.0 | all-reduce | flops 3 | bytes 24 | tf_op jit(solution)/shard_map/psum | solution.py:129
  988.4 42.5 %psum.97 = f32[]{:T(128)} all-reduce(f32[]{:T(128)} %get-tuple-element.299), channel_id=1, replica_groups=mesh['wake'=16,'col'=2] {'wake','col'}, use_global_device_ids=true, to_apply=%region_27.0 | all-reduce | flops 1 | bytes 8 | tf_op jit(solution)/shard_map/psum | solution.py:133
  1031.5 20.9 %all_gather.25 = f32[16384]{0:T(1024)S(1)} all-gather(f32[1024]{0:T(1024)S(1)} %broadcast_divide_fusion.2), channel_id=1, replica_groups=mesh['wake'=16,'col'=2] {'wake'}, dimensions={0}, use_global_device_ids=true | all-gather | bytes 69632 | tf_op jit(solution)/shard_map/all_gather | solution.py:114
  1065.6 36.8 %psum.98 = f32[4]{0:T(128)S(1)} all-reduce(f32[4]{0:T(128)S(1)} %pad_maximum_fusion.4), channel_id=1, replica_groups=mesh['wake'=16,'col'=2] {'wake','col'}, use_global_device_ids=true, to_apply=%region_34.0 | all-reduce | flops 4 | bytes 32 | tf_op jit(solution)/shard_map/psum | solution.py:129
  1106.2 41.6 %psum.99 = f32[]{:T(128)} all-reduce(f32[]{:T(128)} %get-tuple-element.296), channel_id=1, replica_groups=mesh['wake'=16,'col'=2] {'wake','col'}, use_global_device_ids=true, to_apply=%region_36.0 | all-reduce | flops 1 | bytes 8 | tf_op jit(solution)/shard_map/psum | solution.py:133
  1148.5 20.8 %all_gather.26 = f32[16384]{0:T(1024)S(1)} all-gather(f32[1024]{0:T(1024)S(1)} %broadcast_divide_fusion.1), channel_id=1, replica_groups=mesh['wake'=16,'col'=2] {'wake'}, dimensions={0}, use_global_device_ids=true | all-gather | bytes 69632 | tf_op jit(solution)/shard_map/all_gather | solution.py:114
  1182.4 36.8 %psum.100 = f32[5]{0:T(128)S(1)} all-reduce(f32[5]{0:T(128)S(1)} %stack.96), channel_id=1, replica_groups=mesh['wake'=16,'col'=2] {'wake','col'}, use_global_device_ids=true, to_apply=%region_44.0 | all-reduce | flops 5 | bytes 40 | tf_op jit(solution)/shard_map/psum | solution.py:129
  1223.7 42.4 %psum.101 = f32[]{:T(128)} all-reduce(f32[]{:T(128)} %get-tuple-element.293), channel_id=1, replica_groups=mesh['wake'=16,'col'=2] {'wake','col'}, use_global_device_ids=true, to_apply=%region_46.0 | all-reduce | flops 1 | bytes 8 | tf_op jit(solution)/shard_map/psum | solution.py:133
  1266.8 20.9 %all_gather.27 = f32[16384]{0:T(1024)S(1)} all-gather(f32[1024]{0:T(1024)S(1)} %broadcast_divide_fusion), channel_id=1, replica_groups=mesh['wake'=16,'col'=2] {'wake'}, dimensions={0}, use_global_device_ids=true | all-gather | bytes 69632 | tf_op jit(solution)/shard_map/all_gather | solution.py:114
  1302.2 36.8 %psum.102 = f32[6]{0:T(128)S(1)} all-reduce(f32[6]{0:T(128)S(1)} %stack.103), channel_id=1, replica_groups=mesh['wake'=16,'col'=2] {'wake','col'}, use_global_device_ids=true, to_apply=%region_55.0 | all-reduce | flops 6 | bytes 48 | tf_op jit(solution)/shard_map/psum | solution.py:129
  1344.8 41.6 %psum.103 = f32[]{:T(128)} all-reduce(f32[]{:T(128)} %multiply_reduce_fusion.3), channel_id=1, replica_groups=mesh['wake'=16,'col'=2] {'wake','col'}, use_global_device_ids=true, to_apply=%region_57.0 | all-reduce | flops 1 | bytes 8 | tf_op jit(solution)/shard_map/psum | solution.py:133
  (342 shorter events, 355.6 us)
Async XLA Ops:
  0.6 710.9 %copy-start = (f32[1,32,16384]{2,1,0:T(8,128)S(1)}, f32[1,32,16384]{2,1,0:T(8,128)}, u32[]{:S(2)}) copy-start(f32[1,32,16384]{2,1,0:T(8,128)} %param.47) | copy-start | bytes 6291460
  3.5 11.7 collective-permute-start
  44.7 665.1 %copy-start.1 = (f32[16,1,1,128,128]{4,3,2,1,0:T(8,128)S(1)}, f32[16,1,1,128,128]{4,3,2,1,0:T(8,128)}, u32[]{:S(2)}) copy-start(f32[16,1,1,128,128]{4,3,2,1,0:T(8,128)} %param.44) | copy-start | bytes 3145732
  45.6 10.0 copy-start.3
  64.4 10.0 copy-start.3
  83.3 10.0 copy-start.3
  102.1 10.0 copy-start.3
  121.0 10.0 copy-start.3
  139.9 10.0 copy-start.3
  158.7 10.0 copy-start.3
  177.6 10.0 copy-start.3
  196.4 10.0 copy-start.3
  215.3 10.0 copy-start.3
  234.2 10.0 copy-start.3
  253.0 10.0 copy-start.3
  271.9 10.0 copy-start.3
  290.7 10.0 copy-start.3
  309.6 10.0 copy-start.3
  328.4 10.0 copy-start.3
  347.3 10.0 copy-start.3
  366.2 10.0 copy-start.3
  385.0 10.0 copy-start.3
  403.9 10.0 copy-start.3
  422.7 10.0 copy-start.3
  441.6 10.0 copy-start.3
  460.5 10.0 copy-start.3
  479.3 10.0 copy-start.3
  498.2 10.0 copy-start.3
  517.0 10.0 copy-start.3
  535.9 10.0 copy-start.3
  554.8 10.0 copy-start.3
  573.6 10.0 copy-start.3
  592.5 10.0 copy-start.3
  611.3 10.0 copy-start.3
  630.2 10.0 copy-start.3
  648.2 65.1 %copy-start.2 = (f32[1,32,2048]{2,1,0:T(8,128)S(1)}, f32[1,32,2048]{2,1,0:T(8,128)}, u32[]{:S(2)}) copy-start(f32[1,32,2048]{2,1,0:T(8,128)} %param.46) | copy-start | bytes 786436
  648.2 70.4 %copy-start.4 = (f32[1024]{0:T(1024)S(1)}, f32[1024]{0:T(1024)}, u32[]{:S(2)}) copy-start(f32[1024]{0:T(1024)} %param.43) | copy-start | bytes 12292
where the time goes:
time: 1450 us; the launch traced here: 1430 us
  blocking collectives  693 us (48%)
  other arithmetic  598 us (41%)
  local copies, waits for them, and re-layouts  85.1 us (6%)
  between operations  24.4 us (2%)
  matrix products  23.4 us (2%)
    reduce_sum x32, other arithmetic, induce(): near_len = jnp.sqrt(jnp.sum(near_arm * near_arm, axis=0))  295 us
    reduce_sum x32, other arithmetic, induce(): return jnp.sum(factor * normal_part, axis=1)  253 us
    psum x6, blocking collectives, body(): lax.psum(jnp.sum(remainder * remainder), ('wake', 'col'))  252 us
    psum x6, blocking collectives, body(): coeffs = lax.psum(local_dots, ('wake', 'col'))  221 us
    all_gather x6, blocking collectives, body(): column_vec = lax.all_gather(vector, 'wake', axis=0, tiled=True)  126 us
    psum x1, blocking collectives, body(): initial_sq = lax.psum(jnp.sum(right_side * right_side), ('wake', 'col'))  37.1 us
    unnamed x6, blocking collectives  30.1 us
  transfers between devices with their start and end apart: 1, of which 0 were waited for; matrix products, arithmetic and copies ran while one was open for 1% of the time, Pallas kernels for 0%

commit v1 on v0

--- a/solution.py
+++ b/solution.py
@@ -126,7 +126,7 @@
         )
         image_vec = self_term * vector + summed
         local_dots = jnp.stack([jnp.sum(image_vec * member) for member in krylov])
-        coeffs = lax.psum(local_dots, ("wake", "col"))
+        coeffs = lax.psum(lax.psum(local_dots, "col"), "wake")
         remainder = image_vec
         for position in range(column + 1):
             remainder = remainder - coeffs[position] * krylov[position]

time: 1450 us -> 1400 us (0.966)
  blocking collectives: 693 us -> 653 us
    psum x6, blocking collectives: 252 us -> 222 us  [body(): lax.psum(jnp.sum(remainder * remainder), ('wake', 'col'))]
    psum x6 -> x12, blocking collectives: 221 us -> 208 us  [body(): coeffs = lax.psum(lax.psum(local_dots, 'col'), 'wake')]
  transfers between devices with their start and end apart: 1 -> 1, of which waited for: 0 -> 0; matrix products, arithmetic and copies ran while one was open for 1% -> 0% of each run, Pallas kernels for 0% -> 0%
where the time goes in v1:
time: 1400 us; the launch traced here: 1380 us
  blocking collectives  653 us (47%)
  other arithmetic  596 us (43%)
  local copies, waits for them, and re-layouts  85 us (6%)
  between operations  24.4 us (2%)
  matrix products  23.4 us (2%)
    reduce_sum x32, other arithmetic, induce(): near_len = jnp.sqrt(jnp.sum(near_arm * near_arm, axis=0))  295 us
    reduce_sum x32, other arithmetic, induce(): return jnp.sum(factor * normal_part, axis=1)  253 us
    psum x6, blocking collectives, body(): lax.psum(jnp.sum(remainder * remainder), ('wake', 'col'))  222 us
    psum x12, blocking collectives, body(): coeffs = lax.psum(lax.psum(local_dots, 'col'), 'wake')  208 us
    all_gather x6, blocking collectives, body(): column_vec = lax.all_gather(vector, 'wake', axis=0, tiled=True)  129 us
    psum x1, blocking collectives, body(): initial_sq = lax.psum(jnp.sum(right_side * right_side), ('wake', 'col'))  37.1 us
    unnamed x6, blocking collectives  30.1 us
  transfers between devices with their start and end apart: 1, of which 0 were waited for; matrix products, arithmetic and copies ran while one was open for 0% of the time, Pallas kernels for 0%

profile of v1, /device:TPU:0, one launch (start us, length us, event | category | flops | bytes accessed | tf_op | source)
XLA Modules:
  0.0 1383.9 jit_solution(15476005207193162302)
XLA Ops:
  14.1 26.6 %all_gather.21 = f32[7,16384]{1,0:T(8,128)} all-gather(f32[7,1024]{1,0:T(8,128)S(1)} %pad_maximum_fusion), channel_id=1, replica_groups=mesh['wake'=16,'col'=2] {'wake'}, dimensions={1}, use_global_device_ids=true | all-gather | bytes 487424 | tf_op jit(solution)/shard_map/all_gather | solution.py:89
  40.7 603.5 %while.26 = (s32[]{:T(128)}, f32[1024]{0:T(1024)S(1)}, f32[7,16384]{1,0:T(8,128)}, f32[3,1024]{1,0:T(4,128)}, f32[3,1024]{1,0:T(4,128)}, /*index=5*/s32[]{:T(128...) while((s32[]{:T(128)}, f32[1024]{0:T(1024)S(1)}, f32[7,16384]{1,0:T(8,128)}, ...), condition=%wide.region_5.0_spmd.clone, body=%wide.region_0.0_spmd.clone.sunk | while | flops 23593992 | bytes 37906656 | solution.py:99
  41.6 9.2 multiply_reduce_fusion.32
  51.6 7.9 fusion.107
  60.5 9.2 multiply_reduce_fusion.32
  79.3 9.2 multiply_reduce_fusion.32
  89.3 7.9 fusion.107
  98.2 9.2 multiply_reduce_fusion.32
  117.0 9.2 multiply_reduce_fusion.32
  135.9 9.2 multiply_reduce_fusion.32
  145.9 7.9 fusion.107
  154.8 9.2 multiply_reduce_fusion.32
  173.6 9.2 multiply_reduce_fusion.32
  192.5 9.2 multiply_reduce_fusion.32
  202.5 7.9 fusion.107
  211.3 9.2 multiply_reduce_fusion.32
  230.2 9.2 multiply_reduce_fusion.32
  240.2 7.9 fusion.107
  249.1 9.2 multiply_reduce_fusion.32
  267.9 9.2 multiply_reduce_fusion.32
  286.8 9.2 multiply_reduce_fusion.32
  296.8 7.9 fusion.107
  305.6 9.2 multiply_reduce_fusion.32
  324.5 9.2 multiply_reduce_fusion.32
  343.3 9.2 multiply_reduce_fusion.32
  353.4 7.9 fusion.107
  362.2 9.2 multiply_reduce_fusion.32
  381.1 9.2 multiply_reduce_fusion.32
  399.9 9.2 multiply_reduce_fusion.32
  418.8 9.2 multiply_reduce_fusion.32
  437.6 9.2 multiply_reduce_fusion.32
  447.7 7.9 fusion.107
  456.5 9.2 multiply_reduce_fusion.32
  475.4 9.2 multiply_reduce_fusion.32
  494.2 9.2 multiply_reduce_fusion.32
  504.2 7.9 fusion.107
  513.1 9.2 multiply_reduce_fusion.32
  531.9 9.2 multiply_reduce_fusion.32
  550.8 9.2 multiply_reduce_fusion.32
  560.8 7.9 fusion.107
  569.7 9.2 multiply_reduce_fusion.32
  588.5 9.2 multiply_reduce_fusion.32
  598.5 7.9 fusion.107
  607.4 9.2 multiply_reduce_fusion.32
  626.2 9.2 multiply_reduce_fusion.32
  645.5 37.1 %psum.133 = f32[]{:T(128)} all-reduce(f32[]{:T(128)} %multiply_reduce_fusion.30), channel_id=1, replica_groups=mesh['wake'=16,'col'=2] {'wake','col'}, use_global_device_ids=true, to_apply=%region_7.0 | all-reduce | flops 1 | bytes 8 | tf_op jit(solution)/shard_map/psum | solution.py:108
  683.9 21.4 %all_gather.22 = f32[16384]{0:T(1024)S(1)} all-gather(f32[1024]{0:T(1024)S(1)} %get-tuple-element.307), channel_id=1, replica_groups=mesh['wake'=16,'col'=2] {'wake'}, dimensions={0}, use_global_device_ids=true | all-gather | bytes 69632 | tf_op jit(solution)/shard_map/all_gather | solution.py:114
  721.6 30.1 %psum.135 = f32[1]{0:T(128)} all-reduce(f32[1]{0:T(128)} %psum.134), channel_id=1, replica_groups=mesh['wake'=16,'col'=2] {'wake'}, use_global_device_ids=true, to_apply=%region_11.0 | all-reduce | flops 1 | bytes 8 | tf_op jit(solution)/shard_map/psum | solution.py:129
  752.9 37.0 %psum.136 = f32[]{:T(128)} all-reduce(f32[]{:T(128)} %get-tuple-element.305), channel_id=1, replica_groups=mesh['wake'=16,'col'=2] {'wake','col'}, use_global_device_ids=true, to_apply=%region_13.0 | all-reduce | flops 1 | bytes 8 | tf_op jit(solution)/shard_map/psum | solution.py:133
  790.6 21.6 %all_gather.23 = f32[16384]{0:T(1024)S(1)} all-gather(f32[1024]{0:T(1024)S(1)} %broadcast_divide_fusion.4), channel_id=1, replica_groups=mesh['wake'=16,'col'=2] {'wake'}, dimensions={0}, use_global_device_ids=true | all-gather | bytes 69632 | tf_op jit(solution)/shard_map/all_gather | solution.py:114
  829.6 29.5 %psum.138 = f32[2]{0:T(128)S(1)} all-reduce(f32[2]{0:T(128)S(1)} %psum.137), channel_id=1, replica_groups=mesh['wake'=16,'col'=2] {'wake'}, use_global_device_ids=true, to_apply=%region_19.0 | all-reduce | flops 2 | bytes 16 | tf_op jit(solution)/shard_map/psum | solution.py:129
  861.4 37.1 %psum.139 = f32[]{:T(128)} all-reduce(f32[]{:T(128)} %get-tuple-element.302), channel_id=1, replica_groups=mesh['wake'=16,'col'=2] {'wake','col'}, use_global_device_ids=true, to_apply=%region_21.0 | all-reduce | flops 1 | bytes 8 | tf_op jit(solution)/shard_map/psum | solution.py:133
  899.2 21.5 %all_gather.24 = f32[16384]{0:T(1024)S(1)} all-gather(f32[1024]{0:T(1024)S(1)} %broadcast_divide_fusion.3), channel_id=1, replica_groups=mesh['wake'=16,'col'=2] {'wake'}, dimensions={0}, use_global_device_ids=true | all-gather | bytes 69632 | tf_op jit(solution)/shard_map/all_gather | solution.py:114
  938.0 29.5 %psum.141 = f32[3]{0:T(128)S(1)} all-reduce(f32[3]{0:T(128)S(1)} %psum.140), channel_id=1, replica_groups=mesh['wake'=16,'col'=2] {'wake'}, use_global_device_ids=true, to_apply=%region_28.0 | all-reduce | flops 3 | bytes 24 | tf_op jit(solution)/shard_map/psum | solution.py:129
  970.7 37.0 %psum.142 = f32[]{:T(128)} all-reduce(f32[]{:T(128)} %get-tuple-element.299), channel_id=1, replica_groups=mesh['wake'=16,'col'=2] {'wake','col'}, use_global_device_ids=true, to_apply=%region_30.0 | all-reduce | flops 1 | bytes 8 | tf_op jit(solution)/shard_map/psum | solution.py:133
  1008.4 21.5 %all_gather.25 = f32[16384]{0:T(1024)S(1)} all-gather(f32[1024]{0:T(1024)S(1)} %broadcast_divide_fusion.2), channel_id=1, replica_groups=mesh['wake'=16,'col'=2] {'wake'}, dimensions={0}, use_global_device_ids=true | all-gather | bytes 69632 | tf_op jit(solution)/shard_map/all_gather | solution.py:114
  1048.0 29.7 %psum.144 = f32[4]{0:T(128)S(1)} all-reduce(f32[4]{0:T(128)S(1)} %psum.143), channel_id=1, replica_groups=mesh['wake'=16,'col'=2] {'wake'}, use_global_device_ids=true, to_apply=%region_38.0 | all-reduce | flops 4 | bytes 32 | tf_op jit(solution)/shard_map/psum | solution.py:129
  1081.5 37.0 %psum.145 = f32[]{:T(128)} all-reduce(f32[]{:T(128)} %get-tuple-element.296), channel_id=1, replica_groups=mesh['wake'=16,'col'=2] {'wake','col'}, use_global_device_ids=true, to_apply=%region_40.0 | all-reduce | flops 1 | bytes 8 | tf_op jit(solution)/shard_map/psum | solution.py:133
  1119.2 21.5 %all_gather.26 = f32[16384]{0:T(1024)S(1)} all-gather(f32[1024]{0:T(1024)S(1)} %broadcast_divide_fusion.1), channel_id=1, replica_groups=mesh['wake'=16,'col'=2] {'wake'}, dimensions={0}, use_global_device_ids=true | all-gather | bytes 69632 | tf_op jit(solution)/shard_map/all_gather | solution.py:114
  1159.4 29.5 %psum.147 = f32[5]{0:T(128)S(1)} all-reduce(f32[5]{0:T(128)S(1)} %psum.146), channel_id=1, replica_groups=mesh['wake'=16,'col'=2] {'wake'}, use_global_device_ids=true, to_apply=%region_49.0 | all-reduce | flops 5 | bytes 40 | tf_op jit(solution)/shard_map/psum | solution.py:129
  1193.3 37.1 %psum.148 = f32[]{:T(128)} all-reduce(f32[]{:T(128)} %get-tuple-element.293), channel_id=1, replica_groups=mesh['wake'=16,'col'=2] {'wake','col'}, use_global_device_ids=true, to_apply=%region_51.0 | all-reduce | flops 1 | bytes 8 | tf_op jit(solution)/shard_map/psum | solution.py:133
  1231.0 21.5 %all_gather.27 = f32[16384]{0:T(1024)S(1)} all-gather(f32[1024]{0:T(1024)S(1)} %broadcast_divide_fusion), channel_id=1, replica_groups=mesh['wake'=16,'col'=2] {'wake'}, dimensions={0}, use_global_device_ids=true | all-gather | bytes 69632 | tf_op jit(solution)/shard_map/all_gather | solution.py:114
  1271.8 29.5 %psum.150 = f32[6]{0:T(128)S(1)} all-reduce(f32[6]{0:T(128)S(1)} %psum.149), channel_id=1, replica_groups=mesh['wake'=16,'col'=2] {'wake'}, use_global_device_ids=true, to_apply=%region_61.0 | all-reduce | flops 6 | bytes 48 | tf_op jit(solution)/shard_map/psum | solution.py:129
  1306.9 37.1 %psum.151 = f32[]{:T(128)} all-reduce(f32[]{:T(128)} %multiply_reduce_fusion.3), channel_id=1, replica_groups=mesh['wake'=16,'col'=2] {'wake','col'}, use_global_device_ids=true, to_apply=%region_63.0 | all-reduce | flops 1 | bytes 8 | tf_op jit(solution)/shard_map/psum | solution.py:133
  (352 shorter events, 383.6 us)
Async XLA Ops:
  0.6 707.0 %copy-start = (f32[1,32,16384]{2,1,0:T(8,128)S(1)}, f32[1,32,16384]{2,1,0:T(8,128)}, u32[]{:S(2)}) copy-start(f32[1,32,16384]{2,1,0:T(8,128)} %param.47) | copy-start | bytes 6291460
  3.5 7.7 collective-permute-start
  40.7 665.2 %copy-start.1 = (f32[16,1,1,128,128]{4,3,2,1,0:T(8,128)S(1)}, f32[16,1,1,128,128]{4,3,2,1,0:T(8,128)}, u32[]{:S(2)}) copy-start(f32[16,1,1,128,128]{4,3,2,1,0:T(8,128)} %param.44) | copy-start | bytes 3145732
  41.6 10.0 copy-start.3
  60.5 10.0 copy-start.3
  79.3 10.0 copy-start.3
  98.2 10.0 copy-start.3
  117.0 10.0 copy-start.3
  135.9 10.0 copy-start.3
  154.8 10.0 copy-start.3
  173.6 10.0 copy-start.3
  192.5 10.0 copy-start.3
  211.3 10.0 copy-start.3
  230.2 10.0 copy-start.3
  249.0 10.0 copy-start.3
  267.9 10.0 copy-start.3
  286.8 10.0 copy-start.3
  305.6 10.0 copy-start.3
  324.5 10.0 copy-start.3
  343.3 10.0 copy-start.3
  362.2 10.0 copy-start.3
  381.1 10.0 copy-start.3
  399.9 10.0 copy-start.3
  418.8 10.0 copy-start.3
  437.6 10.0 copy-start.3
  456.5 10.0 copy-start.3
  475.4 10.0 copy-start.3
  494.2 10.0 copy-start.3
  513.1 10.0 copy-start.3
  531.9 10.0 copy-start.3
  550.8 10.0 copy-start.3
  569.7 10.0 copy-start.3
  588.5 10.0 copy-start.3
  607.4 10.0 copy-start.3
  626.2 10.0 copy-start.3
  644.2 65.2 %copy-start.2 = (f32[1,32,2048]{2,1,0:T(8,128)S(1)}, f32[1,32,2048]{2,1,0:T(8,128)}, u32[]{:S(2)}) copy-start(f32[1,32,2048]{2,1,0:T(8,128)} %param.46) | copy-start | bytes 786436
  644.2 70.5 %copy-start.4 = (f32[1024]{0:T(1024)S(1)}, f32[1024]{0:T(1024)}, u32[]{:S(2)}) copy-start(f32[1024]{0:T(1024)} %param.43) | copy-start | bytes 12292
  644.2 76.6 %copy-start.6 = (s32[2]{0:T(128)S(1)}, s32[2]{0:T(128)}, u32[]{:S(2)}) copy-start(s32[2]{0:T(128)} %constant.361.clone.1) | copy-start | bytes 28
  709.4 114.0 %copy-start.5 = (s32[2]{0:T(128)S(1)}, s32[2]{0:T(128)}, u32[]{:S(2)}) copy-start(s32[2]{0:T(128)} %constant.362.clone.1) | copy-start | bytes 28
